TPU v7x, 512 devices: a whole 4x4x16 slice. The times are simulated.
512 devices in a mesh: segment: 8 (over y, core), vocab: 64 (over z, x).
Axes of the slice: x: 4, y: 4, z: 16, core: 2. Of those that a mesh axis runs over, the one named last changes fastest.
Arguments:
- hidden: bfloat16 [16384, 8192], P('vocab', 'segment'), may hold values from -160 to 160
- norm_gain: float32 [8192], P('segment'), may hold values from 0.5 to 1.5
- head: bfloat16 [65536, 8192], P('vocab', 'segment'), may hold values from -3 to 3
- allowed: int32 [4, 16384], P(None, 'vocab'), may hold values from 0 to 127, as said below
- target_slot: int32 [16384], P('vocab'), may hold values from 0 to 3
- target_offset: int32 [16384], P('vocab'), may hold values from 0 to 511
Outputs:
- logprob: float32 [16384], P('vocab')
Inputs may be any that keep to these rules, and one draw needn't show every extreme that they name: `allowed`: the 4 blocks of a token are distinct. Among the 256 tokens of one index of vocab, a block is named by at most 16 of them; in every draw some block is named by exactly 16 tokens of every index of vocab.
All inputs are finite; a program needn't handle non-finite values.
Results may differ from a plain program's by a relative error of at most 0.00083.
Values may be sent and summed in bfloat16 or wider, within the bound.
A program may use at most 64 MiB of HBM per device.

v0:
```python
import jax
import jax.numpy as jnp
from jax import lax
from jax.sharding import PartitionSpec as P

D = 8192
BLOCK = 512
A = 4


def block_stats(logits, targets):
    peak_value = jnp.max(logits, axis=-1)
    exp_total = jnp.sum(jnp.exp(logits - peak_value[..., None]), axis=-1)
    column = lax.broadcasted_iota(jnp.int32, logits.shape, logits.ndim - 1)
    target_logit = jnp.sum(
        jnp.where(column == targets[..., None], logits, jnp.zeros_like(logits)), axis=-1
    )
    return (peak_value, exp_total, target_logit)


def per_device(hidden, norm_gain, head, allowed, target_slot, target_offset):
    tok_count = hidden.shape[0]
    slab_width = hidden.shape[1]
    vocab_size = lax.axis_size("vocab")
    blk_dev = head.shape[0] // BLOCK
    blk_count = blk_dev * vocab_size
    capacity = 2 * tok_count * A // blk_count
    widened = hidden.astype(jnp.float32)
    squares = lax.psum(jnp.sum(widened * widened, axis=1), "segment")
    normed = (widened * lax.rsqrt(squares / D + 1e-05)[:, None] * norm_gain[None, :]).astype(
        jnp.bfloat16
    )
    entries = allowed.reshape(-1)
    onehot = (entries[:, None] == jnp.arange(blk_count, dtype=jnp.int32)[None, :]).astype(jnp.int32)
    before = jnp.cumsum(onehot, axis=0) - onehot
    position = jnp.sum(before * onehot, axis=1)
    slot_index = entries * capacity + position
    slot_total = blk_count * capacity
    entry_token = jnp.tile(jnp.arange(tok_count, dtype=jnp.int32), A)
    slot_token = jnp.full((slot_total,), tok_count, jnp.int32).at[slot_index].set(entry_token)
    entry_choice = jnp.repeat(jnp.arange(A, dtype=jnp.int32), tok_count)
    entry_target = jnp.where(
        entry_choice == jnp.tile(target_slot, A), jnp.tile(target_offset, A), -1
    )
    slot_target = jnp.full((slot_total,), -1, jnp.int32).at[slot_index].set(entry_target)
    padded = jnp.concatenate([normed, jnp.zeros((1, slab_width), jnp.bfloat16)], axis=0)
    outgoing = padded[slot_token].reshape(vocab_size, blk_dev, capacity, slab_width)
    incoming, wanted = (
        lax.all_to_all(outgoing, "vocab", split_axis=0, concat_axis=0, tiled=True),
        lax.all_to_all(
            slot_target.reshape(vocab_size, blk_dev, capacity),
            "vocab",
            split_axis=0,
            concat_axis=0,
            tiled=True,
        ),
    )
    weights = head.reshape(blk_dev, BLOCK, slab_width)
    logits = lax.psum(
        jnp.einsum("sbcd,bvd->sbcv", incoming, weights, preferred_element_type=jnp.float32),
        "segment",
    )
    peak_value, exp_total, target_logit = block_stats(logits, wanted)
    peak_value, exp_total, target_logit = (
        lax.all_to_all(peak_value, "vocab", split_axis=0, concat_axis=0, tiled=True),
        lax.all_to_all(exp_total, "vocab", split_axis=0, concat_axis=0, tiled=True),
        lax.all_to_all(target_logit, "vocab", split_axis=0, concat_axis=0, tiled=True),
    )
    peak_value = peak_value.reshape(-1)[slot_index].reshape(A, tok_count)
    exp_total = exp_total.reshape(-1)[slot_index].reshape(A, tok_count)
    target_logit = target_logit.reshape(-1)[slot_index].reshape(A, tok_count)
    largest = jnp.max(peak_value, axis=0)
    log_total = largest + jnp.log(
        jnp.sum(exp_total * jnp.exp(peak_value - largest[None, :]), axis=0)
    )
    return jnp.sum(target_logit, axis=0) - log_total


def solution(mesh):
    return jax.shard_map(
        per_device,
        mesh=mesh,
        in_specs=(
            P("vocab", "segment"),
            P("segment"),
            P("vocab", "segment"),
            P(None, "vocab"),
            P("vocab"),
            P("vocab"),
        ),
        out_specs=P("vocab"),
        check_vma=False,
    )
```

profile of v0, /device:TPU:1, one launch (start us, length us, event | category | flops | bytes accessed | tf_op | source)
XLA Modules:
  0.0 416.2 jit_solution(16631843202107226767)
XLA Ops:
  6.5 0.0 copy-start
  6.5 0.0 copy-start.1
  6.5 0.0 all-reduce.3.cloned.1.call-start
  6.5 0.8 eq.41
  7.4 0.7 multiply_bitcast_fusion
  8.1 0.1 copy.27
  8.2 0.2 fusion.10
  8.5 0.1 copy.28
  8.6 0.7 copy.36
  9.3 0.4 fusion.9
  9.7 4.3 %scatter_custom_fusion.1 = s32[2048]{0:T(1024)S(1)} fusion(s32[1024]{0:T(1024)S(1)} %bitcast.39, s32[1024]{0:T(1024)S(1)} %bitcast.43, s32[]{:T(128)} %constant.7.clone.1), kind=kCustom, calls=%fused_computation.32 | custom fusion | bytes 8196 | tf_op jit(solution)/shard_map/scatter | solution.py:40
  14.0 1.2 fusion.5
  15.2 18.6 %psum.14 = f32[256]{0:T(256)S(1)} all-reduce(f32[256]{0:T(256)S(1)} %fusion.5), channel_id=1, replica_groups=mesh['segment'=8,'vocab'=64] {'segment'}, use_global_device_ids=true, to_apply=%region_5.6 | all-reduce | flops 256 | bytes 2048 | tf_op jit(solution)/shard_map/psum | solution.py:29
  33.9 0.0 copy-done.1
  33.9 0.9 fusion.7
  34.8 9.7 %gather_fusion = bf16[2048,1024]{1,0:T(8,128)(2,1)} fusion(bf16[257,1024]{1,0:T(8,128)(2,1)S(1)} %concatenate.3, s32[2048]{0:T(1024)S(1)} %fusion.13), kind=kCustom, calls=%fused_computation | custom fusion | bytes 8396800 | tf_op jit(solution)/shard_map/gather | solution.py:47
  44.5 196.4 %all_to_all.25 = bf16[64,2,16,1024]{3,2,1,0:T(8,128)(2,1)S(1)} all-to-all(bf16[64,2,16,1024]{3,2,1,0:T(8,128)(2,1)} %bitcast.35), channel_id=1, replica_groups=mesh['segment'=8,'vocab'=64] {'vocab'}, dimensions={0} | all-to-all | bytes 8388608 | tf_op jit(solution)/shard_map/all_to_all | solution.py:49
  240.9 0.0 copy-done
  240.9 4.3 %fusion.2 = f32[64,2,16,512]{3,2,0,1:T(8,128)} fusion(bf16[2,512,1024,1]{2,1,3,0:T(8,128)(2,1)S(1)} %bitcast.34, bf16[64,2,16,1024]{3,2,1,0:T(8,128)(2,1)S(1)} %all_to_all.25), kind=kOutput, calls=%fused_computation.11 | convolution fusion | flops 2147483648 | bytes 10485760 | tf_op jit(solution)/shard_map/sbcd,bvd->sbcv/dot_general | solution.py:60
  245.3 0.0 copy-start.2
  245.3 0.0 copy-start.3
  245.3 0.0 all-reduce.3.cloned.1.call-update
  245.3 0.7 copy-done.2
  246.0 0.0 copy-done.3
  246.0 4.3 %scatter_custom_fusion = s32[2048]{0:T(1024)S(1)} fusion(s32[1024]{0:T(1024)S(1)} %bitcast.40, s32[1024]{0:T(1024)S(1)} %bitcast.44, s32[]{:T(128)} %constant.11.clone.1), kind=kCustom, calls=%fused_computation.37 | custom fusion | bytes 8196 | tf_op jit(solution)/shard_map/scatter | solution.py:45
  250.3 0.1 reshape.85
  250.4 23.6 %all_to_all.26 = s32[64,2,16]{2,1,0:T(2,128)S(1)} all-to-all(s32[64,2,16]{2,1,0:T(2,128)S(1)} %reshape.85), channel_id=1, replica_groups=mesh['segment'=8,'vocab'=64] {'vocab'}, dimensions={0} | all-to-all | bytes 16384 | tf_op jit(solution)/shard_map/all_to_all | solution.py:50
  274.1 55.4 %all-reduce.3.cloned.1.call-done = f32[64,2,16,512]{3,2,0,1:T(8,128)} async-done(((f32[64,2,16,512]{3,2,0,1:T(8,128)}), f32[64,2,16,512]{3,2,0,1:T(8,128)}) %all-reduce.3.cloned.1.call-update) | async-done | bytes 4194320 | tf_op jit(solution)/shard_map/psum | solution.py:59
  329.5 2.5 reduce_max.18
  332.0 3.2 exponential_reduce_fusion
  335.2 0.7 copy.33
  335.8 15.3 %all-to-all-start.4 = ((f32[64,2,16]{2,1,0:T(2,128)}), f32[64,2,16]{2,1,0:T(2,128)S(1)}, u32[]{:S(2)}, u32[]{:S(2)}) async-start(f32[64,2,16]{2,1,0:T(2,128)} %copy.33), calls=%async_computation.4 | async-start | bytes 131072 | tf_op jit(solution)/shard_map/all_to_all | solution.py:66
  351.2 0.7 copy.32
  351.8 13.3 %all-to-all-done.4 = f32[64,2,16]{2,1,0:T(2,128)S(1)} async-done(((f32[64,2,16]{2,1,0:T(2,128)}), f32[64,2,16]{2,1,0:T(2,128)S(1)}, u32[]{:S(2)}, u32[]{:S(2)}) %all-to-all-start.4) | async-done | bytes 8224 | tf_op jit(solution)/shard_map/all_to_all | solution.py:66
  365.2 4.6 %all-to-all-start.3 = ((f32[64,2,16]{2,1,0:T(2,128)}), f32[64,2,16]{2,1,0:T(2,128)S(1)}, u32[]{:S(2)}, u32[]{:S(2)}) async-start(f32[64,2,16]{2,1,0:T(2,128)} %copy.32), calls=%async_computation.3 | async-start | bytes 131072 | tf_op jit(solution)/shard_map/all_to_all | solution.py:65
  369.8 0.7 copy.31
  370.5 13.3 %all-to-all-done.3 = f32[64,2,16]{2,1,0:T(2,128)S(1)} async-done(((f32[64,2,16]{2,1,0:T(2,128)}), f32[64,2,16]{2,1,0:T(2,128)S(1)}, u32[]{:S(2)}, u32[]{:S(2)}) %all-to-all-start.3) | async-done | bytes 8224 | tf_op jit(solution)/shard_map/all_to_all | solution.py:65
  383.8 4.6 %all-to-all-start.2 = ((f32[64,2,16]{2,1,0:T(2,128)}), f32[64,2,16]{2,1,0:T(2,128)S(1)}, u32[]{:S(2)}, u32[]{:S(2)}) async-start(f32[64,2,16]{2,1,0:T(2,128)} %copy.31), calls=%async_computation.2 | async-start | bytes 131072 | tf_op jit(solution)/shard_map/all_to_all | solution.py:67
  388.4 0.1 reshape.92
  388.5 6.2 %gather_fusion.3 = f32[1024]{0:T(1024)S(1)} fusion(f32[2048]{0:T(1024)S(1)} %reshape.92, s32[1024]{0:T(1024)S(1)} %broadcast_clamp_fusion), kind=kCustom, calls=%fused_computation.3 | custom fusion | bytes 12288 | tf_op jit(solution)/shard_map/gather | solution.py:70
  394.7 0.1 reshape.90
  394.8 6.2 %gather_fusion.2 = f32[1024]{0:T(1024)S(1)} fusion(f32[2048]{0:T(1024)S(1)} %reshape.90, s32[1024]{0:T(1024)S(1)} %broadcast_clamp_fusion), kind=kCustom, calls=%fused_computation.2 | custom fusion | bytes 12288 | tf_op jit(solution)/shard_map/gather | solution.py:69
  401.0 1.4 all-to-all-done.2
  402.4 0.1 reshape.88
  402.5 6.2 %gather_fusion.1 = f32[1024]{0:T(1024)S(1)} fusion(f32[2048]{0:T(1024)S(1)} %reshape.88, s32[1024]{0:T(1024)S(1)} %broadcast_clamp_fusion), kind=kCustom, calls=%fused_computation.1 | custom fusion | bytes 12288 | tf_op jit(solution)/shard_map/gather | solution.py:71
  408.7 0.6 add_subtract_fusion
  (21 shorter events, 0.3 us)
Async XLA Ops:
  6.5 234.4 %copy-start = (bf16[1024,1024]{1,0:T(8,128)(2,1)S(1)}, bf16[1024,1024]{1,0:T(8,128)(2,1)}, u32[]{:S(2)}) copy-start(bf16[1024,1024]{1,0:T(8,128)(2,1)} %param.8) | copy-start | bytes 6291460
  6.5 27.4 %copy-start.1 = (bf16[256,1024]{1,0:T(8,128)(2,1)S(1)}, bf16[256,1024]{1,0:T(8,128)(2,1)}, u32[]{:S(2)}) copy-start(bf16[256,1024]{1,0:T(8,128)(2,1)} %param.6) | copy-start | bytes 1572868
  6.5 322.9 %all-reduce.3.cloned.1.call-start = ((), (), s32[]{:S(2)}) async-start(), calls=%async_computation.5 | async-start | bytes 8388608 | tf_op jit(solution)/shard_map/psum | solution.py:59
  245.3 0.7 copy-start.2
  245.3 0.7 copy-start.3
  335.8 29.3 %all-to-all-start.4 = ((f32[64,2,16]{2,1,0:T(2,128)}), f32[64,2,16]{2,1,0:T(2,128)S(1)}, u32[]{:S(2)}, u32[]{:S(2)}) async-start(f32[64,2,16]{2,1,0:T(2,128)} %copy.33), calls=%async_computation.4 | async-start | bytes 131072 | tf_op jit(solution)/shard_map/all_to_all | solution.py:66
  365.2 18.6 %all-to-all-start.3 = ((f32[64,2,16]{2,1,0:T(2,128)}), f32[64,2,16]{2,1,0:T(2,128)S(1)}, u32[]{:S(2)}, u32[]{:S(2)}) async-start(f32[64,2,16]{2,1,0:T(2,128)} %copy.32), calls=%async_computation.3 | async-start | bytes 131072 | tf_op jit(solution)/shard_map/all_to_all | solution.py:65
  383.8 18.6 %all-to-all-start.2 = ((f32[64,2,16]{2,1,0:T(2,128)}), f32[64,2,16]{2,1,0:T(2,128)S(1)}, u32[]{:S(2)}, u32[]{:S(2)}) async-start(f32[64,2,16]{2,1,0:T(2,128)} %copy.31), calls=%async_computation.2 | async-start | bytes 131072 | tf_op jit(solution)/shard_map/all_to_all | solution.py:67
Sparse Core Ops, SparseCore 0:
  245.4 83.9 all-reduce.2
where the time goes:
time: 420 us; the launch traced here: 416 us
  blocking collectives  239 us (57%)
  waiting for transfers between devices  83.5 us (20%)
  local copies, waits for them, and re-layouts  41.8 us (10%)
  starting transfers between devices  24.5 us (6%)
  between operations  13.6 us (3%)
  other arithmetic  9.78 us (2%)
  matrix products  4.34 us (1%)
    all_to_all x1, blocking collectives, per_device(): lax.all_to_all(outgoing, 'vocab', split_axis=0, concat_axis=0, tiled=True)  196 us
    psum x1, waiting for transfers between devices, per_device(): lax.psum(jnp.einsum('sbcd,bvd->sbcv', incoming, weights, preferred_elemen...  55.4 us
    all_to_all x1, blocking collectives, per_device(): lax.all_to_all(slot_target.reshape(vocab_size, blk_dev, capacity), 'vocab...  23.6 us
    psum x1, blocking collectives, per_device(): squares = lax.psum(jnp.sum(widened * widened, axis=1), 'segment')  18.6 us
    all_to_all x1, starting transfers between devices, per_device(): lax.all_to_all(exp_total, 'vocab', split_axis=0, concat_axis=0, tiled=True)  15.3 us
    all_to_all x1, waiting for transfers between devices, per_device(): lax.all_to_all(peak_value, 'vocab', split_axis=0, concat_axis=0, tiled=True)  13.3 us
    all_to_all x1, waiting for transfers between devices, per_device(): lax.all_to_all(exp_total, 'vocab', split_axis=0, concat_axis=0, tiled=True)  13.3 us
    gather x1, local copies, waits for them, and re-layouts, per_device(): padded[slot_token].reshape(vocab_size, blk_dev, capacity, slab_width)  9.67 us
  transfers between devices with their start and end apart: 4, of which 4 were waited for; matrix products, arithmetic and copies ran while one was open for 4% of the time, Pallas kernels for 0%

commit v1 on v0

v1 whole, which is shorter than its diff:
```python
import functools

import jax
import jax.numpy as jnp
from jax import lax
from jax.experimental import pallas as pl
from jax.experimental.pallas import tpu as pltpu
from jax.sharding import PartitionSpec as P

D = 8192
BLOCK = 512
A = 4
CAP = 16
NZ = 16
NX = 4
TOK = 256
SLAB = 1024
F32 = jnp.float32
BF16 = jnp.bfloat16
ROUND_A = ((0, 2, 0, 3),)
ROUND_B = ((0, 2, 3, 5), (2, 3, 0, 5))
ROUND_C = ((0, 3, 5, 6), (3, 4, 0, 6))
ROUND_D = ((0, 4, 6, 7),)
ROUND_E = ((0, 4, 7, 8),)
ROUNDS = ROUND_A + ROUND_B + ROUND_C + ROUND_D + ROUND_E


def kernel(
    hid,
    gain,
    head,
    allowed,
    tslot,
    toff,
    out,
    X,
    M,
    H,
    G,
    Pp,
    Pr,
    St,
    Rs,
    Rr,
    rcode,
    Sx,
    E,
    acc,
    xs,
    xr,
    ms,
    mr,
    hs,
    hr,
    ps,
    pr,
    ss,
    sr,
    es,
    er,
    ts,
    tr,
    own,
):
    seg = lax.axis_index("segment")
    v = lax.axis_index("vocab")
    z = v // NX
    x = lax.rem(v, NX)
    my_i = seg // 4
    my_h = lax.rem(seg // 2, 2)
    my_d = lax.rem(seg, 2)

    def at_z(step):
        return lax.rem(z + step + NZ, NZ) * NX + x

    def at_x(step):
        return z * NX + lax.rem(x + step + NX, NX)

    def push(src, dst, send, recv, s, d):
        return pltpu.make_async_remote_copy(
            src_ref=src,
            dst_ref=dst,
            send_sem=send,
            recv_sem=recv,
            device_id=(s, d),
            device_id_type=pl.DeviceIdType.MESH,
        )

    own_slab = pltpu.make_async_copy(hid, X.at[0, 7], own.at[0])
    own_slab.start()
    own_head = [
        pltpu.make_async_copy(head.at[pl.ds(i * BLOCK, BLOCK)], H.at[0, i], own.at[1 + i])
        for i in range(2)
    ]
    for c in own_head:
        c.start()

    barrier = pltpu.get_barrier_semaphore()
    for d in (at_z(1), at_z(-1), at_x(1), at_x(-1)):
        pl.semaphore_signal(
            barrier, inc=1, device_id=(seg, d), device_id_type=pl.DeviceIdType.MESH
        )
    for rel in range(1, 8):
        pl.semaphore_signal(
            barrier,
            inc=1,
            device_id=(lax.rem(seg + rel, 8), v),
            device_id_type=pl.DeviceIdType.MESH,
        )
    pl.semaphore_wait(barrier, 11)

    half = TOK // 2
    sides = (at_z(1), at_z(-1))

    def slab(k, d, c):
        rows = pl.ds(c * half, half)
        src = hid.at[rows] if k == 0 else X.at[d, k - 1, rows]
        dst = X.at[1, 7, rows] if k == 7 else X.at[d, k, rows]
        return push(src, dst, xs.at[d, k, c], xr.at[d, k, c], seg, sides[d])

    def meta(k, d):
        src = M.at[0, 7] if k == 0 else M.at[d, k - 1]
        dst = M.at[1, 7] if k == 7 else M.at[d, k]
        return push(src, dst, ms.at[d, k], mr.at[d, k], seg, sides[d])

    for c in range(2):
        for d in range(2):
            slab(0, d, c).start()

    first, second = head.at[pl.ds(0, BLOCK)], head.at[pl.ds(BLOCK, BLOCK)]

    def block(w, i):
        src = ((first, second), (second, first), (H.at[1, 0], H.at[1, 1]))[w - 1][i]
        return push(src, H.at[w, i], hs.at[w, i], hr.at[w, i], seg, at_x(1 - 2 * i))

    for i in range(2):
        block(1, i).start()

    tokens = lax.broadcasted_iota(jnp.int32, (TOK, TOK), 0)
    later = lax.broadcasted_iota(jnp.int32, (TOK, TOK), 1)
    upper = jnp.where(tokens < later, 1.0, 0.0).astype(BF16)
    blocks = lax.broadcasted_iota(jnp.int32, (128, TOK), 0)
    seen = jnp.zeros((128, 1), F32)
    codes = []
    for j in range(A):
        named = blocks == allowed[pl.ds(j, 1), :]
        hot = jnp.where(named, 1.0, 0.0)
        before = jnp.dot(hot.astype(BF16), upper, preferred_element_type=F32) + seen
        place = jnp.sum(jnp.where(named, before, 0.0), axis=0, keepdims=True)
        codes.append((allowed[pl.ds(j, 1), :] * CAP).astype(F32) + place)
        seen = seen + jnp.sum(hot, axis=1, keepdims=True)
    target = codes[0]
    for j in range(1, A):
        target = jnp.where(tslot[...] == j, codes[j], target)
    offset = toff[...].astype(F32)

    slot = lax.broadcasted_iota(jnp.int32, (CAP, TOK), 0)
    left, right, across = (lax.rem(x + s, NX) for s in (3, 1, 2))
    for i in range(2):
        for w in range(4):
            column = (x, (left, right)[i], (left, right)[i], across)[w]
            odd = (i, i, 1 - i, i)[w]
            which = (z * 8 + column * 2 + odd) * CAP
            rcode[i, pl.ds(w * CAP, CAP), :] = (slot + which).astype(F32)

    own_slab.wait()
    squares = jnp.zeros((TOK, 128), F32)
    for c in range(SLAB // 128):
        part = X[0, 7, :, pl.ds(c * 128, 128)].astype(F32)
        squares = squares + part * part
    Sx[0] = jnp.sum(squares.T.reshape(16, 8, TOK), axis=0)

    def square(rel):
        return push(
            Sx.at[0], Sx.at[rel], ss.at[rel], sr.at[rel], lax.rem(seg + rel, 8), v
        )

    for rel in range(1, 8):
        square(rel).start()
    total = Sx[0]
    for rel in range(1, 8):
        square(rel).wait_recv()
        total = total + Sx[rel]
    scale = lax.rsqrt(jnp.sum(total, axis=0, keepdims=True) * (1.0 / D) + 1e-05)
    M[0, 7] = jnp.concatenate(codes + [scale, target, offset, offset], axis=0)
    for d in range(2):
        meta(0, d).start()

    def gather(k, d):
        hit = None
        for i in range(2):
            info = M[d, k]
            rows = rcode[i]
            hit = rows == info[0:1, :]
            for j in range(1, A):
                hit = hit | (rows == info[j : j + 1, :])
            pick = jnp.where(hit, 1.0, 0.0).astype(BF16)
            picked = jnp.dot(pick, X[d, k], preferred_element_type=F32)
            size = jnp.sum(jnp.where(hit, info[4:5, :], 0.0), axis=1, keepdims=True)
            normed = (picked * size * gain[...]).astype(BF16)
            for w in range(4):
                G[w, i, k, d] = normed[w * CAP : (w + 1) * CAP]

    def products(w0, w1, k0, k1):
        count = k1 - k0

        def one(n, carry):
            w, i = n // 2, lax.rem(n, 2)
            rows = G[w, i, pl.ds(k0, count)].reshape(count * 2 * CAP, SLAB)
            logits = lax.dot_general(
                rows, H[w, i], (((1,), (1,)), ((), ())), preferred_element_type=F32
            )
            logits = logits.reshape(count, 2, CAP, BLOCK).astype(BF16)
            for d in range(2):
                for h in range(2):
                    Pp[4 * i + 2 * h + d, pl.ds(k0, count), w] = logits[
                        :, d, :, 256 * h : 256 * (h + 1)
                    ]
            return carry

        lax.fori_loop(2 * w0, 2 * w1, one, 0)

    def partial(r, rel):
        w0, w1, k0, k1 = ROUNDS[r]
        dest = lax.rem(seg + rel, 8)
        part = (pl.ds(k0, k1 - k0), pl.ds(w0, w1 - w0))
        return push(
            Pp.at[(dest, *part)],
            Pr.at[(rel, *part)],
            ps.at[r, rel],
            pr.at[r, rel],
            dest,
            v,
        )

    def send_round(rounds):
        for r in rounds:
            products(*ROUNDS[r])

            def one(rel, carry, r=r):
                partial(r, rel).start()
                return carry

            lax.fori_loop(1, 8, one, 0)

    def stats(rounds):
        for r in rounds:
            w0, w1, k0, k1 = ROUNDS[r]
            n = (w1 - w0) * CAP

            def arrive(rel, carry, r=r):
                partial(r, rel).wait_recv()
                return carry

            lax.fori_loop(1, 8, arrive, 0)

            def one(k, carry, w0=w0, w1=w1, n=n):
                span = pl.ds(w0, w1 - w0)
                logits = Pp[seg, k, span].reshape(n, 256).astype(F32)
                for rel in range(1, 8):
                    logits = logits + Pr[rel, k, span].reshape(n, 256).astype(F32)
                info = M[my_d, k]
                rows = rcode[my_i, pl.ds(w0 * CAP, n), :]
                wanted = jnp.sum(
                    jnp.where(rows == info[5:6, :], info[6:7, :] + 1.0, 0.0),
                    axis=1,
                    keepdims=True,
                )
                column = lax.broadcasted_iota(jnp.int32, (n, 256), 1) + 256 * my_h + 1
                peak = jnp.max(logits, axis=1, keepdims=True)
                mass = jnp.sum(jnp.exp(logits - peak), axis=1, keepdims=True)
                goal = jnp.sum(
                    jnp.where(column.astype(F32) == wanted, logits, 0.0),
                    axis=1,
                    keepdims=True,
                )
                lane = lax.broadcasted_iota(jnp.int32, (n, 128), 1)
                St[k, pl.ds(w0 * CAP, n), :] = jnp.where(
                    lane == 0, peak, jnp.where(lane == 1, mass, goal)
                )
                return carry

            lax.fori_loop(k0, k1, one, 0)

    def report(k):
        step = jnp.where(my_d == 0, -(k + 1), k + 1)
        return push(Rs.at[k], Rr.at[k], ts.at[k], tr.at[k], seg, at_z(step))

    def turn(k):
        rows = St[k]
        Rs[k] = jnp.concatenate([rows, rows], axis=0).T[0:8]

    acc[...] = jnp.zeros((16, TOK), F32)

    def collect(k, step):
        plane = lax.rem(z + step + NZ, NZ) - z
        rows = rcode[my_i] + (plane * 128).astype(F32)
        columns = jnp.concatenate([Rr[k]] * 16, axis=0).T
        for j in range(A):
            match = rows == M[0, 7, j : j + 1, :]
            for q in range(3):
                acc[pl.ds(4 * q + j, 1), :] += jnp.sum(
                    jnp.where(match, columns[0:64, q : q + 1], 0.0), axis=0, keepdims=True
                )

    gather(7, 0)
    for c in own_head:
        c.wait()

    for k in range(7):
        for c in range(2):
            for d in range(2):
                slab(k, d, c).wait_recv()
                if k < 6 or c == d:
                    slab(k + 1, d, c).start()
        for d in range(2):
            meta(k, d).wait_recv()
            if k < 6 or d == 0:
                meta(k + 1, d).start()
        for d in range(2):
            gather(k, d)
        if k == 1:
            for i in range(2):
                block(1, i).wait()
                block(2, i).start()
        if k == 2:
            send_round((0,))
        if k == 3:
            for i in range(2):
                block(2, i).wait()
                block(3, i).start()
            stats((0,))
        if k == 4:
            send_round((1, 2))
        if k == 5:
            for i in range(2):
                block(3, i).wait()
            send_round((3, 4))
        if k == 6:
            send_round((5,))
            stats((1, 2))

    slab(7, 0, 0).wait_recv()
    slab(7, 1, 1).wait_recv()
    meta(7, 0).wait_recv()
    gather(7, 1)
    send_round((6,))
    stats((3, 4))
    for k in range(6):
        turn(k)
        report(k).start()
    stats((5,))
    turn(6)
    report(6).start()
    stats((6,))
    turn(7)

    @pl.when(my_d == 0)
    def _():
        Rr[7] = Rs[7]

    @pl.when(my_d == 1)
    def _():
        report(7).start()

    for k in range(7):
        report(k).wait_recv()
        collect(k, jnp.where(my_d == 0, k + 1, -(k + 1)))

    @pl.when(my_d == 1)
    def _():
        report(7).wait()

    collect(7, jnp.where(my_d == 0, 0, -8))

    peak, mass, goal = (acc[4 * q : 4 * q + 4] for q in range(3))
    have = mass > 0.5
    largest = jnp.max(jnp.where(have, peak, -1e30), axis=0, keepdims=True)
    weight = jnp.where(have, jnp.exp(jnp.where(have, peak - largest, 0.0)), 0.0)
    E[0] = jnp.concatenate(
        [
            largest,
            jnp.sum(mass * weight, axis=0, keepdims=True),
            jnp.sum(goal, axis=0, keepdims=True),
            jnp.zeros((5, TOK), F32),
        ],
        axis=0,
    )

    def share(rel):
        return push(E.at[0], E.at[rel], es.at[rel], er.at[rel], lax.rem(seg + rel, 8), v)

    for rel in range(1, 8):
        share(rel).start()
    for rel in range(1, 8):
        share(rel).wait_recv()
    top = E[0, 0:1]
    for rel in range(1, 8):
        top = jnp.maximum(top, E[rel, 0:1])
    mass = jnp.zeros((1, TOK), F32)
    goal = jnp.zeros((1, TOK), F32)
    for rel in range(8):
        mass = mass + E[rel, 1:2] * jnp.exp(E[rel, 0:1] - top)
        goal = goal + E[rel, 2:3]
    out[...] = goal - (top + jnp.log(mass))

    for rel in range(1, 8):
        share(rel).wait_send()
        square(rel).wait_send()
    for k in range(8):
        for d in range(2):
            for c in range(2):
                if k < 7 or c == d:
                    slab(k, d, c).wait_send()
            if k < 7 or d == 0:
                meta(k, d).wait_send()
    for k in range(7):
        report(k).wait_send()
    for r in range(len(ROUNDS)):

        def left_here(rel, carry, r=r):
            partial(r, rel).wait_send()
            return carry

        lax.fori_loop(1, 8, left_here, 0)


def per_device(hidden, norm_gain, head, allowed, target_slot, target_offset):
    vmem = pl.BlockSpec(memory_space=pltpu.VMEM)
    hbm = pl.BlockSpec(memory_space=pl.ANY)
    dma = pltpu.SemaphoreType.DMA
    out = pl.pallas_call(
        kernel,
        out_shape=jax.ShapeDtypeStruct((1, TOK), F32),
        in_specs=[hbm, vmem, hbm, vmem, vmem, vmem],
        out_specs=vmem,
        scratch_shapes=[
            pltpu.VMEM((2, 8, TOK, SLAB), BF16),
            pltpu.VMEM((2, 8, 8, TOK), F32),
            pltpu.VMEM((4, 2, BLOCK, SLAB), BF16),
            pltpu.VMEM((4, 2, 8, 2, CAP, SLAB), BF16),
            pltpu.VMEM((8, 8, 4, CAP, 256), BF16),
            pltpu.VMEM((8, 8, 4, CAP, 256), BF16),
            pltpu.VMEM((8, 64, 128), F32),
            pltpu.VMEM((8, 8, 128), F32),
            pltpu.VMEM((8, 8, 128), F32),
            pltpu.VMEM((2, 64, TOK), F32),
            pltpu.VMEM((8, 8, TOK), F32),
            pltpu.VMEM((8, 8, TOK), F32),
            pltpu.VMEM((16, TOK), F32),
            dma((2, 8, 2)),
            dma((2, 8, 2)),
            dma((2, 8)),
            dma((2, 8)),
            dma((4, 2)),
            dma((4, 2)),
            dma((len(ROUNDS), 8)),
            dma((len(ROUNDS), 8)),
            dma((8,)),
            dma((8,)),
            dma((8,)),
            dma((8,)),
            dma((8,)),
            dma((8,)),
            dma((3,)),
        ],
        compiler_params=pltpu.CompilerParams(
            collective_id=0, has_side_effects=True, vmem_limit_bytes=56 * 2**20
        ),
    )(
        hidden,
        norm_gain.reshape(1, SLAB),
        head,
        allowed,
        target_slot.reshape(1, TOK),
        target_offset.reshape(1, TOK),
    )
    return out.reshape(TOK)


def solution(mesh):
    return jax.shard_map(
        per_device,
        mesh=mesh,
        in_specs=(
            P("vocab", "segment"),
            P("segment"),
            P("vocab", "segment"),
            P(None, "vocab"),
            P("vocab"),
            P("vocab"),
        ),
        out_specs=P("vocab"),
        check_vma=False,
    )
```

time: 420 us -> 126 us (0.30)
  blocking collectives: 239 us -> 0 us
  Pallas kernels: 0 us -> 125 us
  waiting for transfers between devices: 83.5 us -> 0 us
  local copies, waits for them, and re-layouts: 41.8 us -> 1.24 us
  starting transfers between devices: 24.5 us -> 0 us
  between operations: 13.6 us -> 0.01 us
  other arithmetic: 9.78 us -> 0 us
  matrix products: 4.34 us -> 0 us
    all_to_all x2 -> x0, blocking collectives: 220 us -> none  [the longest x1 196 us: per_device(): lax.all_to_all(outgoing, 'vocab', split_axis=0, concat_axis=0, tiled=True)]
    pallas_call x0 -> x1, Pallas kernels: none -> 125 us  [per_device(): pl.pallas_call(kernel, out_shape=jax.ShapeDtypeStruct((1, TOK), F32), in_...]
    psum x1 -> x0, waiting for transfers between devices: 55.4 us -> none  [per_device(): lax.psum(jnp.einsum('sbcd,bvd->sbcv', incoming, weights, preferred_elemen...]
    gather x4 -> x0, local copies, waits for them, and re-layouts: 28.1 us -> none  [the longest x1 9.67 us: per_device(): padded[slot_token].reshape(vocab_size, blk_dev, capacity, slab_width)]
    all_to_all x3 -> x0, waiting for transfers between devices: 28.1 us -> none  [the longest x1 13.3 us: per_device(): lax.all_to_all(peak_value, 'vocab', split_axis=0, concat_axis=0, tiled=True)]
    all_to_all x3 -> x0, starting transfers between devices: 24.5 us -> none  [the longest x1 15.3 us: per_device(): lax.all_to_all(exp_total, 'vocab', split_axis=0, concat_axis=0, tiled=True)]
    psum x1 -> x0, blocking collectives: 18.6 us -> none  [per_device(): squares = lax.psum(jnp.sum(widened * widened, axis=1), 'segment')]
    scatter x2 -> x0, local copies, waits for them, and re-layouts: 8.63 us -> none  [the longest x1 4.32 us: per_device(): jnp.full((slot_total,), tok_count, jnp.int32).at[slot_index]]
  transfers between devices with their start and end apart: 4 -> 0, of which waited for: 4 -> 0; matrix products, arithmetic and copies ran while one was open for 4% -> 0% of each run, Pallas kernels for 0% -> 0%
where the time goes in v1:
time: 126 us
  Pallas kernels  125 us (99%)
    pallas_call x1, Pallas kernels, per_device(): pl.pallas_call(kernel, out_shape=jax.ShapeDtypeStruct((1, TOK), F32), in_...  125 us

profile of v1, /device:TPU:1, one launch (start us, length us, event | category | flops | bytes accessed | tf_op | source)
XLA Modules:
  0.0 126.1 jit_solution(8506338630656185729)
XLA Ops:
  0.0 124.8 %shard_map.64 = f32[1,256]{1,0:T(1,128)} custom-call(bf16[256,1024]{1,0:T(8,128)(2,1)} %hid.1, f32[1,1024]{1,0:T(1,128)} %bitcast.4, bf16[1024,1024]{1,0:T(8,128)(2,1)} %head.1, s32[4,256]{1,0:T(4,128)} %allowed.1, s32[1,256]{1,0:T(1,128)} %bitcast.6, s32[1,256]{1,0:T(1,128)} %bitcast.7), custom_call_target="tpu_custom_call" | custom-call | tf_op jit(solution)/shard_map/pallas_call | solution.py:432
  124.8 1.2 copy.8

commit v2 on v1

v2 whole, which is shorter than its diff:
```python
import functools

import jax
import jax.numpy as jnp
from jax import lax
from jax.experimental import pallas as pl
from jax.experimental.pallas import tpu as pltpu
from jax.sharding import PartitionSpec as P

D = 8192
BLOCK = 512
A = 4
CAP = 16
NZ = 16
NX = 4
TOK = 256
SLAB = 1024
F32 = jnp.float32
BF16 = jnp.bfloat16
ROUND_A = ((0, 2, 1, 4, None), (0, 2, 0, 1, 0))
ROUND_B = ((0, 2, 4, 6, None), (2, 3, 1, 6, None), (2, 3, 0, 1, 0))
ROUND_C = ((0, 3, 6, 7, None), (3, 4, 1, 7, None), (3, 4, 0, 1, 0))
ROUND_D = ((0, 4, 7, 8, None),)
ROUND_E = ((0, 2, 0, 1, 1), (2, 4, 0, 1, 1))
ROUNDS = ROUND_A + ROUND_B + ROUND_C + ROUND_D + ROUND_E


def kernel(
    hid,
    gain,
    head,
    allowed,
    tslot,
    toff,
    out,
    X,
    F,
    N,
    Z,
    M,
    H,
    G,
    Pp,
    Pr,
    St,
    Rs,
    Rr,
    rcode,
    Sx,
    E,
    acc,
    xs,
    xr,
    fs,
    fr,
    ms,
    mr,
    hs,
    hr,
    ps,
    pr,
    ss,
    sr,
    es,
    er,
    ts,
    tr,
    own,
):
    seg = lax.axis_index("segment")
    v = lax.axis_index("vocab")
    z = v // NX
    x = lax.rem(v, NX)
    my_i = seg // 4
    my_h = lax.rem(seg // 2, 2)
    my_d = lax.rem(seg, 2)

    def at_z(step):
        return lax.rem(z + step + NZ, NZ) * NX + x

    def at_x(step):
        return z * NX + lax.rem(x + step + NX, NX)

    def push(src, dst, send, recv, s, d):
        return pltpu.make_async_remote_copy(
            src_ref=src,
            dst_ref=dst,
            send_sem=send,
            recv_sem=recv,
            device_id=(s, d),
            device_id_type=pl.DeviceIdType.MESH,
        )

    own_slab = pltpu.make_async_copy(hid, X.at[0, 0], own.at[0])
    own_slab.start()
    own_head = [
        pltpu.make_async_copy(head.at[pl.ds(i * BLOCK, BLOCK)], H.at[0, i], own.at[1 + i])
        for i in range(2)
    ]
    for c in own_head:
        c.start()

    barrier = pltpu.get_barrier_semaphore()
    for d in (at_z(1), at_z(-1), at_x(1), at_x(-1)):
        pl.semaphore_signal(
            barrier, inc=1, device_id=(seg, d), device_id_type=pl.DeviceIdType.MESH
        )
    for rel in range(1, 8):
        pl.semaphore_signal(
            barrier,
            inc=1,
            device_id=(lax.rem(seg + rel, 8), v),
            device_id_type=pl.DeviceIdType.MESH,
        )
    pl.semaphore_wait(barrier, 11)

    half = TOK // 2
    sides = (at_z(1), at_z(-1))

    def slab(k, d, c):
        rows = pl.ds(c * half, half)
        src = hid.at[rows] if k == 1 else X.at[d, k - 1, rows]
        return push(
            src, X.at[d, k, rows], xs.at[d, k, c], xr.at[d, k, c], seg, sides[d]
        )

    def far(n, d):
        src = (F.at[d, 0:64], F.at[d, 64:192], N.at[d, 0:64])[n]
        dst = (N.at[d, 0:64], N.at[d, 64:192], Z.at[d])[n]
        return push(src, dst, fs.at[d, n], fr.at[d, n], seg, sides[d])

    def meta(k, d):
        src = M.at[0, 0] if k == 1 else M.at[d, k - 1]
        dst = M.at[1, 0] if k == 8 else M.at[d, k]
        return push(src, dst, ms.at[d, k - 1], mr.at[d, k - 1], seg, sides[d])

    for c in range(2):
        for d in range(2):
            slab(1, d, c).start()

    first, second = head.at[pl.ds(0, BLOCK)], head.at[pl.ds(BLOCK, BLOCK)]

    def block(w, i):
        src = ((first, second), (second, first), (H.at[1, 0], H.at[1, 1]))[w - 1][i]
        return push(src, H.at[w, i], hs.at[w, i], hr.at[w, i], seg, at_x(1 - 2 * i))

    for i in range(2):
        block(1, i).start()

    tokens = lax.broadcasted_iota(jnp.int32, (TOK, TOK), 0)
    later = lax.broadcasted_iota(jnp.int32, (TOK, TOK), 1)
    upper = jnp.where(tokens < later, 1.0, 0.0).astype(BF16)
    blocks = lax.broadcasted_iota(jnp.int32, (128, TOK), 0)
    seen = jnp.zeros((128, 1), F32)
    codes = []
    for j in range(A):
        named = blocks == allowed[pl.ds(j, 1), :]
        hot = jnp.where(named, 1.0, 0.0)
        before = jnp.dot(hot.astype(BF16), upper, preferred_element_type=F32) + seen
        place = jnp.sum(jnp.where(named, before, 0.0), axis=0, keepdims=True)
        codes.append((allowed[pl.ds(j, 1), :] * CAP).astype(F32) + place)
        seen = seen + jnp.sum(hot, axis=1, keepdims=True)
    target = codes[0]
    for j in range(1, A):
        target = jnp.where(tslot[...] == j, codes[j], target)
    offset = toff[...].astype(F32)

    slot = lax.broadcasted_iota(jnp.int32, (CAP, TOK), 0)
    left, right, across = (lax.rem(x + s, NX) for s in (3, 1, 2))
    for i in range(2):
        for w in range(4):
            column = (x, (left, right)[i], (left, right)[i], across)[w]
            odd = (i, i, 1 - i, i)[w]
            which = (z * 8 + column * 2 + odd) * CAP
            rcode[i, pl.ds(w * CAP, CAP), :] = (slot + which).astype(F32)

    own_slab.wait()
    squares = jnp.zeros((TOK, 128), F32)
    for c in range(SLAB // 128):
        part = X[0, 0, :, pl.ds(c * 128, 128)].astype(F32)
        squares = squares + part * part
    Sx[0] = jnp.sum(squares.T.reshape(16, 8, TOK), axis=0)

    def square(rel):
        return push(
            Sx.at[0], Sx.at[rel], ss.at[rel], sr.at[rel], lax.rem(seg + rel, 8), v
        )

    for rel in range(1, 8):
        square(rel).start()
    total = Sx[0]
    for rel in range(1, 8):
        square(rel).wait_recv()
        total = total + Sx[rel]
    scale = lax.rsqrt(jnp.sum(total, axis=0, keepdims=True) * (1.0 / D) + 1e-05)
    M[0, 0] = jnp.concatenate(codes + [scale, target, offset, offset], axis=0)
    for d in range(2):
        meta(1, d).start()

    def hits(info, i, step):
        rows = rcode[i]
        if step is not None:
            rows = rows + ((lax.rem(z + step + NZ, NZ) - z) * 128).astype(F32)
        hit = rows == info[0:1, :]
        for j in range(1, A):
            hit = hit | (rows == info[j : j + 1, :])
        return hit

    def choose(hit):
        return jnp.where(hit, 1.0, 0.0).astype(BF16)

    def keep(k, d, i, info, hit, picked):
        size = jnp.sum(jnp.where(hit, info[4:5, :], 0.0), axis=1, keepdims=True)
        normed = (picked * size * gain[...]).astype(BF16)
        for w in range(4):
            G[w, i, k, d] = normed[w * CAP : (w + 1) * CAP]

    def gather(k, d):
        info = M[d, k]
        for i in range(2):
            hit = hits(info, i, None)
            picked = jnp.dot(choose(hit), X[d, k], preferred_element_type=F32)
            keep(k, d, i, info, hit, picked)

    def compact(d):
        info = M[d, 6]
        step = 1 - 2 * d
        pick = jnp.concatenate(
            [
                choose(hits(info, d, 2 * step)),
                choose(hits(info, 0, step)),
                choose(hits(info, 1, step)),
            ],
            axis=0,
        )
        F[d] = jnp.dot(pick, X[d, 6], preferred_element_type=F32).astype(BF16)

    def arrived(k, d, i, rows):
        info = M[d, k]
        keep(k, d, i, info, hits(info, i, None), rows.astype(F32))

    def spread(w, i, k0, count, logits):
        for d in range(2):
            for h in range(2):
                Pp[4 * i + 2 * h + d, pl.ds(k0, count), w] = logits[
                    :, d, :, 256 * h : 256 * (h + 1)
                ]

    def multiply(rows, w, i):
        return lax.dot_general(
            rows, H[w, i], (((1,), (1,)), ((), ())), preferred_element_type=F32
        )

    def products(w0, w1, k0, k1):
        count = k1 - k0

        def one(n, carry):
            w, i = n // 2, lax.rem(n, 2)
            rows = G[w, i, pl.ds(k0, count)].reshape(count * 2 * CAP, SLAB)
            logits = multiply(rows, w, i).reshape(count, 2, CAP, BLOCK).astype(BF16)
            spread(w, i, k0, count, logits)
            return carry

        lax.fori_loop(2 * w0, 2 * w1, one, 0)

    def products_flat(w0, w1, k):
        for w in range(w0, w1):
            for i in range(2):
                logits = multiply(G[w, i, k].reshape(2 * CAP, SLAB), w, i)
                spread(w, i, k, 1, logits.reshape(1, 2, CAP, BLOCK).astype(BF16))

    def products_last(w0, w1):
        for w in range(w0, w1):
            for i in range(2):
                logits = multiply(G[w, i, 0, 1], w, i).astype(BF16)
                for h in range(2):
                    Pp[4 * i + 2 * h + 1, 0, w] = logits[:, 256 * h : 256 * (h + 1)]

    def partial(r, rel):
        w0, w1, k0, k1, _ = ROUNDS[r]
        dest = lax.rem(seg + rel, 8)
        part = (pl.ds(k0, k1 - k0), pl.ds(w0, w1 - w0))
        return push(
            Pp.at[(dest, *part)],
            Pr.at[(rel, *part)],
            ps.at[r, rel],
            pr.at[r, rel],
            dest,
            v,
        )

    def each_peer(r, act):
        side = ROUNDS[r][4]

        def one(rel, carry):
            if side is None:
                act(partial(r, rel))
            else:

                @pl.when(lax.rem(seg + rel, 2) == side)
                def _():
                    act(partial(r, rel))

            return carry

        lax.fori_loop(1, 8, one, 0)

    def send(rounds):
        for r in rounds:
            each_peer(r, lambda copy: copy.start())

    def sent(rounds):
        for r in rounds:
            each_peer(r, lambda copy: copy.wait_send())

    def stats(rounds):
        for r in rounds:
            side = ROUNDS[r][4]
            if side is None:
                stats_of(r)
            else:
                pl.when(my_d == side)(functools.partial(stats_of, r))

    def stats_of(r):
        w0, w1, k0, k1, _ = ROUNDS[r]
        n = (w1 - w0) * CAP

        def arrive(rel, carry):
            partial(r, rel).wait_recv()
            return carry

        lax.fori_loop(1, 8, arrive, 0)

        def one(k, carry):
            span = pl.ds(w0, w1 - w0)
            logits = Pp[seg, k, span].reshape(n, 256).astype(F32)
            for rel in range(1, 8):
                logits = logits + Pr[rel, k, span].reshape(n, 256).astype(F32)
            info = M[my_d, k]
            rows = rcode[my_i, pl.ds(w0 * CAP, n), :]
            wanted = jnp.sum(
                jnp.where(rows == info[5:6, :], info[6:7, :] + 1.0, 0.0),
                axis=1,
                keepdims=True,
            )
            column = lax.broadcasted_iota(jnp.int32, (n, 256), 1) + 256 * my_h + 1
            peak = jnp.max(logits, axis=1, keepdims=True)
            mass = jnp.sum(jnp.exp(logits - peak), axis=1, keepdims=True)
            goal = jnp.sum(
                jnp.where(column.astype(F32) == wanted, logits, 0.0),
                axis=1,
                keepdims=True,
            )
            lane = lax.broadcasted_iota(jnp.int32, (n, 128), 1)
            St[k, pl.ds(w0 * CAP, n), :] = jnp.where(
                lane == 0, peak, jnp.where(lane == 1, mass, goal)
            )
            return carry

        if k1 - k0 == 1:
            one(k0, 0)
        else:
            lax.fori_loop(k0, k1, one, 0)

    def report(k):
        step = jnp.where(my_d == 0, -k, k) if k else 8
        return push(Rs.at[k], Rr.at[k], ts.at[k], tr.at[k], seg, at_z(step))

    def turn(k):
        rows = St[k]
        Rs[k] = jnp.concatenate([rows, rows], axis=0).T[0:8]

    acc[...] = jnp.zeros((16, TOK), F32)

    def collect(k, step):
        plane = lax.rem(z + step + NZ, NZ) - z
        rows = rcode[my_i] + (plane * 128).astype(F32)
        columns = jnp.concatenate([Rr[k]] * 16, axis=0).T
        for j in range(A):
            match = rows == M[0, 0, j : j + 1, :]
            for q in range(3):
                acc[pl.ds(4 * q + j, 1), :] += jnp.sum(
                    jnp.where(match, columns[0:64, q : q + 1], 0.0), axis=0, keepdims=True
                )

    gather(0, 0)
    for w in range(4):
        for i in range(2):
            G[w, i, 0, 1] = jnp.zeros((CAP, SLAB), BF16)
    for c in own_head:
        c.wait()

    for k in range(1, 6):
        for d in range(2):
            slab(k, d, 0).wait_recv()
            slab(k + 1, d, 0).start()
        for d in range(2):
            slab(k, d, 1).wait_recv()
            meta(k, d).wait_recv()
            meta(k + 1, d).start()
            slab(k + 1, d, 1).start()
        for d in range(2):
            gather(k, d)
        if k == 2:
            for i in range(2):
                block(1, i).wait()
                block(2, i).start()
        if k == 3:
            products(0, 2, 0, 4)
            send((0, 1))
        if k == 4:
            for i in range(2):
                block(2, i).wait()
                block(3, i).start()
        if k == 5:
            products(0, 2, 4, 6)
            send((2,))
            products(2, 3, 0, 6)
            send((3, 4))
            stats((0, 1))

    for d in range(2):
        slab(6, d, 0).wait_recv()
    for d in range(2):
        slab(6, d, 1).wait_recv()
        meta(6, d).wait_recv()
        meta(7, d).start()
        compact(d)
        far(0, d).start()
        far(1, d).start()
    for d in range(2):
        gather(6, d)
    products(0, 3, 6, 7)
    send((5,))
    for d in range(2):
        meta(7, d).wait_recv()
        far(0, d).wait_recv()
        if d == 0:
            meta(8, d).start()
        far(2, d).start()
    for i in range(2):
        block(3, i).wait()
    products(3, 4, 0, 7)
    send((6, 7))
    stats((2, 3, 4))

    for d in range(2):
        far(1, d).wait_recv()
        for i in range(2):
            arrived(7, d, i, N[d, 64 + 64 * i : 128 + 64 * i])
    products_flat(0, 4, 7)
    send((8,))

    meta(8, 0).wait_recv()
    for d in range(2):
        far(2, d).wait_recv()
        arrived(0, 1, d, Z[d])
    products_last(0, 2)
    send((9,))
    products_last(2, 4)
    send((10,))

    stats((5, 6, 7))
    for k in range(1, 7):
        turn(k)
        report(k).start()
    stats((8,))
    turn(7)
    report(7).start()
    stats((9, 10))
    turn(0)

    @pl.when(my_d == 0)
    def _():
        Rr[0] = Rs[0]

    @pl.when(my_d == 1)
    def _():
        report(0).start()

    for k in range(1, 7):
        for d in range(2):
            for c in range(2):
                slab(k, d, c).wait_send()
    for k in range(1, 9):
        for d in range(2 if k < 8 else 1):
            meta(k, d).wait_send()
    for d in range(2):
        for n in range(3):
            far(n, d).wait_send()
    for rel in range(1, 8):
        square(rel).wait_send()
    sent(range(len(ROUNDS)))

    for k in range(1, 8):
        report(k).wait_recv()
        collect(k, jnp.where(my_d == 0, k, -k))

    @pl.when(my_d == 1)
    def _():
        report(0).wait_recv()

    collect(0, jnp.where(my_d == 0, 0, -8))

    peak, mass, goal = (acc[4 * q : 4 * q + 4] for q in range(3))
    have = mass > 0.5
    largest = jnp.max(jnp.where(have, peak, -1e30), axis=0, keepdims=True)
    weight = jnp.where(have, jnp.exp(jnp.where(have, peak - largest, 0.0)), 0.0)
    E[0] = jnp.concatenate(
        [
            largest,
            jnp.sum(mass * weight, axis=0, keepdims=True),
            jnp.sum(goal, axis=0, keepdims=True),
            jnp.zeros((5, TOK), F32),
        ],
        axis=0,
    )

    def share(rel):
        return push(E.at[0], E.at[rel], es.at[rel], er.at[rel], lax.rem(seg + rel, 8), v)

    for rel in range(1, 8):
        share(rel).start()
    for k in range(1, 8):
        report(k).wait_send()

    @pl.when(my_d == 1)
    def _():
        report(0).wait_send()

    for rel in range(1, 8):
        share(rel).wait_recv()
    top = E[0, 0:1]
    for rel in range(1, 8):
        top = jnp.maximum(top, E[rel, 0:1])
    mass = jnp.zeros((1, TOK), F32)
    goal = jnp.zeros((1, TOK), F32)
    for rel in range(8):
        mass = mass + E[rel, 1:2] * jnp.exp(E[rel, 0:1] - top)
        goal = goal + E[rel, 2:3]
    out[...] = goal - (top + jnp.log(mass))
    for rel in range(1, 8):
        share(rel).wait_send()


def per_device(hidden, norm_gain, head, allowed, target_slot, target_offset):
    vmem = pl.BlockSpec(memory_space=pltpu.VMEM)
    hbm = pl.BlockSpec(memory_space=pl.ANY)
    dma = pltpu.SemaphoreType.DMA
    out = pl.pallas_call(
        kernel,
        out_shape=jax.ShapeDtypeStruct((1, TOK), F32),
        in_specs=[hbm, vmem, hbm, vmem, vmem, vmem],
        out_specs=vmem,
        scratch_shapes=[
            pltpu.VMEM((2, 7, TOK, SLAB), BF16),
            pltpu.VMEM((2, 192, SLAB), BF16),
            pltpu.VMEM((2, 192, SLAB), BF16),
            pltpu.VMEM((2, 64, SLAB), BF16),
            pltpu.VMEM((2, 8, 8, TOK), F32),
            pltpu.VMEM((4, 2, BLOCK, SLAB), BF16),
            pltpu.VMEM((4, 2, 8, 2, CAP, SLAB), BF16),
            pltpu.VMEM((8, 8, 4, CAP, 256), BF16),
            pltpu.VMEM((8, 8, 4, CAP, 256), BF16),
            pltpu.VMEM((8, 64, 128), F32),
            pltpu.VMEM((8, 8, 128), F32),
            pltpu.VMEM((8, 8, 128), F32),
            pltpu.VMEM((2, 64, TOK), F32),
            pltpu.VMEM((8, 8, TOK), F32),
            pltpu.VMEM((8, 8, TOK), F32),
            pltpu.VMEM((16, TOK), F32),
            dma((2, 7, 2)),
            dma((2, 7, 2)),
            dma((2, 3)),
            dma((2, 3)),
            dma((2, 8)),
            dma((2, 8)),
            dma((4, 2)),
            dma((4, 2)),
            dma((len(ROUNDS), 8)),
            dma((len(ROUNDS), 8)),
            dma((8,)),
            dma((8,)),
            dma((8,)),
            dma((8,)),
            dma((8,)),
            dma((8,)),
            dma((3,)),
        ],
        compiler_params=pltpu.CompilerParams(
            collective_id=0, has_side_effects=True, vmem_limit_bytes=56 * 2**20
        ),
    )(
        hidden,
        norm_gain.reshape(1, SLAB),
        head,
        allowed,
        target_slot.reshape(1, TOK),
        target_offset.reshape(1, TOK),
    )
    return out.reshape(TOK)


def solution(mesh):
    return jax.shard_map(
        per_device,
        mesh=mesh,
        in_specs=(
            P("vocab", "segment"),
            P("segment"),
            P("vocab", "segment"),
            P(None, "vocab"),
            P("vocab"),
            P("vocab"),
        ),
        out_specs=P("vocab"),
        check_vma=False,
    )
```

time: 126 us -> 120 us (0.952)
  Pallas kernels: 125 us -> 118 us
    pallas_call x1, Pallas kernels: 125 us -> 118 us  [per_device(): pl.pallas_call(kernel, out_shape=jax.ShapeDtypeStruct((1, TOK), F32), in_...]
where the time goes in v2:
time: 120 us
  Pallas kernels  118 us (98%)
  local copies, waits for them, and re-layouts  1.24 us (1%)
    pallas_call x1, Pallas kernels, per_device(): pl.pallas_call(kernel, out_shape=jax.ShapeDtypeStruct((1, TOK), F32), in_...  118 us

profile of v2, /device:TPU:1, one launch (start us, length us, event | category | flops | bytes accessed | tf_op | source)
XLA Modules:
  0.0 119.6 jit_solution(2552824367293011831)
XLA Ops:
  0.0 118.4 %shard_map.64 = f32[1,256]{1,0:T(1,128)} custom-call(bf16[256,1024]{1,0:T(8,128)(2,1)} %hid.1, f32[1,1024]{1,0:T(1,128)} %bitcast.4, bf16[1024,1024]{1,0:T(8,128)(2,1)} %head.1, s32[4,256]{1,0:T(4,128)} %allowed.1, s32[1,256]{1,0:T(1,128)} %bitcast.6, s32[1,256]{1,0:T(1,128)} %bitcast.7), custom_call_target="tpu_custom_call" | custom-call | tf_op jit(solution)/shard_map/pallas_call | solution.py:550
  118.4 1.2 %copy.8 = f32[256]{0:T(256)} copy(f32[256]{0:T(256)} %bitcast.5) | data formatting | bytes 2048

commit v3 on v2

--- a/solution.py
+++ b/solution.py
@@ -34,10 +34,10 @@
     toff,
     out,
     X,
-    F,
-    N,
+    XS,
     Z,
     M,
+    MS,
     H,
     G,
     Pp,
@@ -45,14 +45,14 @@
     St,
     Rs,
     Rr,
+    Qs,
+    Qr,
     rcode,
     Sx,
     E,
     acc,
     xs,
     xr,
-    fs,
-    fr,
     ms,
     mr,
     hs,
@@ -65,6 +65,8 @@
     er,
     ts,
     tr,
+    qs,
+    qr,
     own,
 ):
     seg = lax.axis_index("segment")
@@ -112,41 +114,6 @@
             device_id=(lax.rem(seg + rel, 8), v),
             device_id_type=pl.DeviceIdType.MESH,
         )
-    pl.semaphore_wait(barrier, 11)
-
-    half = TOK // 2
-    sides = (at_z(1), at_z(-1))
-
-    def slab(k, d, c):
-        rows = pl.ds(c * half, half)
-        src = hid.at[rows] if k == 1 else X.at[d, k - 1, rows]
-        return push(
-            src, X.at[d, k, rows], xs.at[d, k, c], xr.at[d, k, c], seg, sides[d]
-        )
-
-    def far(n, d):
-        src = (F.at[d, 0:64], F.at[d, 64:192], N.at[d, 0:64])[n]
-        dst = (N.at[d, 0:64], N.at[d, 64:192], Z.at[d])[n]
-        return push(src, dst, fs.at[d, n], fr.at[d, n], seg, sides[d])
-
-    def meta(k, d):
-        src = M.at[0, 0] if k == 1 else M.at[d, k - 1]
-        dst = M.at[1, 0] if k == 8 else M.at[d, k]
-        return push(src, dst, ms.at[d, k - 1], mr.at[d, k - 1], seg, sides[d])
-
-    for c in range(2):
-        for d in range(2):
-            slab(1, d, c).start()
-
-    first, second = head.at[pl.ds(0, BLOCK)], head.at[pl.ds(BLOCK, BLOCK)]
-
-    def block(w, i):
-        src = ((first, second), (second, first), (H.at[1, 0], H.at[1, 1]))[w - 1][i]
-        return push(src, H.at[w, i], hs.at[w, i], hr.at[w, i], seg, at_x(1 - 2 * i))
-
-    for i in range(2):
-        block(1, i).start()
-
     tokens = lax.broadcasted_iota(jnp.int32, (TOK, TOK), 0)
     later = lax.broadcasted_iota(jnp.int32, (TOK, TOK), 1)
     upper = jnp.where(tokens < later, 1.0, 0.0).astype(BF16)
@@ -174,29 +141,6 @@
             which = (z * 8 + column * 2 + odd) * CAP
             rcode[i, pl.ds(w * CAP, CAP), :] = (slot + which).astype(F32)
 
-    own_slab.wait()
-    squares = jnp.zeros((TOK, 128), F32)
-    for c in range(SLAB // 128):
-        part = X[0, 0, :, pl.ds(c * 128, 128)].astype(F32)
-        squares = squares + part * part
-    Sx[0] = jnp.sum(squares.T.reshape(16, 8, TOK), axis=0)
-
-    def square(rel):
-        return push(
-            Sx.at[0], Sx.at[rel], ss.at[rel], sr.at[rel], lax.rem(seg + rel, 8), v
-        )
-
-    for rel in range(1, 8):
-        square(rel).start()
-    total = Sx[0]
-    for rel in range(1, 8):
-        square(rel).wait_recv()
-        total = total + Sx[rel]
-    scale = lax.rsqrt(jnp.sum(total, axis=0, keepdims=True) * (1.0 / D) + 1e-05)
-    M[0, 0] = jnp.concatenate(codes + [scale, target, offset, offset], axis=0)
-    for d in range(2):
-        meta(1, d).start()
-
     def hits(info, i, step):
         rows = rcode[i]
         if step is not None:
@@ -209,6 +153,101 @@
     def choose(hit):
         return jnp.where(hit, 1.0, 0.0).astype(BF16)
 
+    named = jnp.concatenate(codes, axis=0)
+    own_slab.wait()
+    picks = []
+    for d in range(2):
+        step = 1 - 2 * d
+
+        def marked(hit):
+            return jnp.max(jnp.where(hit, 1.0, 0.0), axis=0, keepdims=True)
+
+        last = marked(hits(named, d, 8))
+        near = jnp.maximum(
+            marked(hits(named, 0, 7 * step)), marked(hits(named, 1, 7 * step))
+        )
+        near = near * (1.0 - last)
+        rest = 1.0 - last - near
+        classes = jnp.concatenate([last, near, rest, jnp.zeros((13, TOK), F32)], axis=0)
+        rank = jnp.dot(classes.astype(BF16), upper, preferred_element_type=F32)
+        n_last = jnp.sum(last, axis=1, keepdims=True)
+        n_near = jnp.sum(near, axis=1, keepdims=True)
+        position = (
+            last * rank[0:1]
+            + near * (n_last + rank[1:2])
+            + rest * (n_last + n_near + rank[2:3])
+        )
+        pick = jnp.where(tokens.astype(F32) == position, 1.0, 0.0)
+        picks.append(pick)
+        for c in range(2):
+            rows = slice(c * 128, (c + 1) * 128)
+            XS[d, rows] = jnp.dot(
+                pick[rows].astype(BF16), X[0, 0], preferred_element_type=F32
+            ).astype(BF16)
+    for d in range(2):
+        X[d, 7, 192:256] = jnp.zeros((64, SLAB), BF16)
+        Z[d, 64:128] = jnp.zeros((64, SLAB), BF16)
+
+    pl.semaphore_wait(barrier, 11)
+
+    sides = (at_z(1), at_z(-1))
+
+    def slab(k, d, c):
+        begin, size = ((0, 64), (64, 64), (128, 64))[c] if k == 7 else (c * 128, 128)
+        if k == 8:
+            begin, size = 0, 64
+        rows = pl.ds(begin, size)
+        src = XS.at[d, rows] if k == 1 else X.at[d, k - 1, rows]
+        dst = Z.at[d, rows] if k == 8 else X.at[d, k, rows]
+        return push(src, dst, xs.at[d, k, c], xr.at[d, k, c], seg, sides[d])
+
+    def meta(k, d):
+        src = MS.at[d] if k == 1 else M.at[d, k - 1]
+        return push(src, M.at[d, k], ms.at[d, k], mr.at[d, k], seg, sides[d])
+
+    for c in range(2):
+        for d in range(2):
+            slab(1, d, c).start()
+
+    first, second = head.at[pl.ds(0, BLOCK)], head.at[pl.ds(BLOCK, BLOCK)]
+
+    def block(w, i):
+        src = ((first, second), (second, first), (H.at[1, 0], H.at[1, 1]))[w - 1][i]
+        return push(src, H.at[w, i], hs.at[w, i], hr.at[w, i], seg, at_x(1 - 2 * i))
+
+    for i in range(2):
+        block(1, i).start()
+
+    squares = jnp.zeros((TOK, 128), F32)
+    for c in range(SLAB // 128):
+        part = X[0, 0, :, pl.ds(c * 128, 128)].astype(F32)
+        squares = squares + part * part
+    Sx[0] = jnp.sum(squares.T.reshape(16, 8, TOK), axis=0)
+
+    def square(rel):
+        return push(
+            Sx.at[0], Sx.at[rel], ss.at[rel], sr.at[rel], lax.rem(seg + rel, 8), v
+        )
+
+    for rel in range(1, 8):
+        square(rel).start()
+    total = Sx[0]
+    for rel in range(1, 8):
+        square(rel).wait_recv()
+        total = total + Sx[rel]
+    scale = lax.rsqrt(jnp.sum(total, axis=0, keepdims=True) * (1.0 / D) + 1e-05)
+    info = jnp.concatenate(codes + [scale, target, offset, offset], axis=0)
+    M[0, 0] = info
+    for d in range(2):
+        MS[d] = lax.dot_general(
+            info,
+            picks[d],
+            (((1,), (1,)), ((), ())),
+            precision=lax.Precision.HIGHEST,
+            preferred_element_type=F32,
+        )
+        meta(1, d).start()
+
     def keep(k, d, i, info, hit, picked):
         size = jnp.sum(jnp.where(hit, info[4:5, :], 0.0), axis=1, keepdims=True)
         normed = (picked * size * gain[...]).astype(BF16)
@@ -222,22 +261,12 @@
             picked = jnp.dot(choose(hit), X[d, k], preferred_element_type=F32)
             keep(k, d, i, info, hit, picked)
 
-    def compact(d):
-        info = M[d, 6]
-        step = 1 - 2 * d
-        pick = jnp.concatenate(
-            [
-                choose(hits(info, d, 2 * step)),
-                choose(hits(info, 0, step)),
-                choose(hits(info, 1, step)),
-            ],
-            axis=0,
-        )
-        F[d] = jnp.dot(pick, X[d, 6], preferred_element_type=F32).astype(BF16)
-
-    def arrived(k, d, i, rows):
-        info = M[d, k]
-        keep(k, d, i, info, hits(info, i, None), rows.astype(F32))
+    def gather_last():
+        for i in range(2):
+            info = M[i, 8]
+            hit = hits(info, i, None)
+            picked = jnp.dot(choose(hit)[:, 0:128], Z[i], preferred_element_type=F32)
+            keep(0, 1, i, info, hit, picked)
 
     def spread(w, i, k0, count, logits):
         for d in range(2):
@@ -331,12 +360,14 @@
 
         lax.fori_loop(1, 8, arrive, 0)
 
+        last = r >= len(ROUNDS) - len(ROUND_E)
+
         def one(k, carry):
             span = pl.ds(w0, w1 - w0)
             logits = Pp[seg, k, span].reshape(n, 256).astype(F32)
             for rel in range(1, 8):
                 logits = logits + Pr[rel, k, span].reshape(n, 256).astype(F32)
-            info = M[my_d, k]
+            info = M[my_i if last else my_d, 8 if last else k]
             rows = rcode[my_i, pl.ds(w0 * CAP, n), :]
             wanted = jnp.sum(
                 jnp.where(rows == info[5:6, :], info[6:7, :] + 1.0, 0.0),
@@ -363,7 +394,7 @@
             lax.fori_loop(k0, k1, one, 0)
 
     def report(k):
-        step = jnp.where(my_d == 0, -k, k) if k else 8
+        step = jnp.where(my_d == 0, -k, k)
         return push(Rs.at[k], Rr.at[k], ts.at[k], tr.at[k], seg, at_z(step))
 
     def turn(k):
@@ -421,23 +452,22 @@
 
     for d in range(2):
         slab(6, d, 0).wait_recv()
+        slab(7, d, 0).start()
+        slab(7, d, 1).start()
     for d in range(2):
         slab(6, d, 1).wait_recv()
         meta(6, d).wait_recv()
         meta(7, d).start()
-        compact(d)
-        far(0, d).start()
-        far(1, d).start()
+        slab(7, d, 2).start()
     for d in range(2):
         gather(6, d)
     products(0, 3, 6, 7)
     send((5,))
     for d in range(2):
+        slab(7, d, 0).wait_recv()
         meta(7, d).wait_recv()
-        far(0, d).wait_recv()
-        if d == 0:
-            meta(8, d).start()
-        far(2, d).start()
+        meta(8, d).start()
+        slab(8, d, 0).start()
     for i in range(2):
         block(3, i).wait()
     products(3, 4, 0, 7)
@@ -445,16 +475,17 @@
     stats((2, 3, 4))
 
     for d in range(2):
-        far(1, d).wait_recv()
-        for i in range(2):
-            arrived(7, d, i, N[d, 64 + 64 * i : 128 + 64 * i])
+        slab(7, d, 1).wait_recv()
+        slab(7, d, 2).wait_recv()
+    for d in range(2):
+        gather(7, d)
     products_flat(0, 4, 7)
     send((8,))
 
-    meta(8, 0).wait_recv()
-    for d in range(2):
-        far(2, d).wait_recv()
-        arrived(0, 1, d, Z[d])
+    for d in range(2):
+        slab(8, d, 0).wait_recv()
+        meta(8, d).wait_recv()
+    gather_last()
     products_last(0, 2)
     send((9,))
     products_last(2, 4)
@@ -467,27 +498,36 @@
     stats((8,))
     turn(7)
     report(7).start()
-    stats((9, 10))
-    turn(0)
+
+    def finish(rel):
+        return push(
+            Qs, Qr.at[2 * my_i + my_h], qs.at[rel], qr.at[2 * my_i + my_h],
+            lax.rem(seg + rel, 8), at_z(8),
+        )
 
     @pl.when(my_d == 0)
     def _():
+        turn(0)
         Rr[0] = Rs[0]
+
+    stats((9, 10))
 
     @pl.when(my_d == 1)
     def _():
-        report(0).start()
-
-    for k in range(1, 7):
+        rows = St[0]
+        turned = jnp.concatenate([rows, rows], axis=0).T
+        lane = lax.broadcasted_iota(jnp.int32, (1, 128), 1)
+        Qs[...] = jnp.concatenate(
+            [jnp.where(lane < 64, turned[0:1], turned[1:2]), turned[2:3]], axis=0
+        )
+        for rel in range(8):
+            finish(rel).start()
+
+    for k in range(1, 9):
         for d in range(2):
-            for c in range(2):
+            for c in range(2 if k < 7 else (3, 1)[k - 7]):
                 slab(k, d, c).wait_send()
-    for k in range(1, 9):
-        for d in range(2 if k < 8 else 1):
             meta(k, d).wait_send()
-    for d in range(2):
-        for n in range(3):
-            far(n, d).wait_send()
     for rel in range(1, 8):
         square(rel).wait_send()
     sent(range(len(ROUNDS)))
@@ -496,11 +536,9 @@
         report(k).wait_recv()
         collect(k, jnp.where(my_d == 0, k, -k))
 
-    @pl.when(my_d == 1)
+    @pl.when(my_d == 0)
     def _():
-        report(0).wait_recv()
-
-    collect(0, jnp.where(my_d == 0, 0, -8))
+        collect(0, 0)
 
     peak, mass, goal = (acc[4 * q : 4 * q + 4] for q in range(3))
     have = mass > 0.5
@@ -524,23 +562,58 @@
     for k in range(1, 8):
         report(k).wait_send()
 
-    @pl.when(my_d == 1)
-    def _():
-        report(0).wait_send()
-
     for rel in range(1, 8):
         share(rel).wait_recv()
+    for n in range(4):
+        push(Qs, Qr.at[n], qs.at[n], qr.at[n], seg, at_z(8)).wait_recv()
+
+    stacked = jnp.concatenate([Qr[n] for n in range(4)], axis=0)
+    columns = jnp.concatenate([stacked] * 16, axis=0).T
+    last = []
+    plane = ((lax.rem(z + 8, NZ) - z) * 128).astype(F32)
+    for i in range(2):
+        first, second = 4 * i, 4 * i + 2
+        peaks = [columns[0:64, n : n + 1] for n in (first, second)]
+        peak = jnp.maximum(peaks[0], peaks[1])
+        mass = columns[64:128, first : first + 1] * jnp.exp(peaks[0] - peak)
+        mass = mass + columns[64:128, second : second + 1] * jnp.exp(peaks[1] - peak)
+        goal = columns[0:64, first + 1 : first + 2] + columns[0:64, second + 1 : second + 2]
+        last.append((rcode[i] + plane, peak, mass, goal))
+    found = []
+    for j in range(A):
+        rows = M[0, 0, j : j + 1, :]
+        sums = [jnp.zeros((1, TOK), F32)] * 3
+        for codes_of, *values in last:
+            match = codes_of == rows
+            sums = [
+                s + jnp.sum(jnp.where(match, value, 0.0), axis=0, keepdims=True)
+                for s, value in zip(sums, values)
+            ]
+        found.append(sums)
+
     top = E[0, 0:1]
     for rel in range(1, 8):
         top = jnp.maximum(top, E[rel, 0:1])
+    for peak, mass, _ in found:
+        top = jnp.maximum(top, jnp.where(mass > 0.5, peak, -1e30))
     mass = jnp.zeros((1, TOK), F32)
     goal = jnp.zeros((1, TOK), F32)
     for rel in range(8):
         mass = mass + E[rel, 1:2] * jnp.exp(E[rel, 0:1] - top)
         goal = goal + E[rel, 2:3]
+    for a_peak, a_mass, a_goal in found:
+        here = a_mass > 0.5
+        weight = jnp.exp(jnp.where(here, a_peak - top, 0.0))
+        mass = mass + jnp.where(here, a_mass * weight, 0.0)
+        goal = goal + a_goal
     out[...] = goal - (top + jnp.log(mass))
     for rel in range(1, 8):
         share(rel).wait_send()
+
+    @pl.when(my_d == 1)
+    def _():
+        for rel in range(8):
+            finish(rel).wait_send()
 
 
 def per_device(hidden, norm_gain, head, allowed, target_slot, target_offset):
@@ -553,11 +626,11 @@
         in_specs=[hbm, vmem, hbm, vmem, vmem, vmem],
         out_specs=vmem,
         scratch_shapes=[
-            pltpu.VMEM((2, 7, TOK, SLAB), BF16),
-            pltpu.VMEM((2, 192, SLAB), BF16),
-            pltpu.VMEM((2, 192, SLAB), BF16),
-            pltpu.VMEM((2, 64, SLAB), BF16),
-            pltpu.VMEM((2, 8, 8, TOK), F32),
+            pltpu.VMEM((2, 8, TOK, SLAB), BF16),
+            pltpu.VMEM((2, TOK, SLAB), BF16),
+            pltpu.VMEM((2, 128, SLAB), BF16),
+            pltpu.VMEM((2, 9, 8, TOK), F32),
+            pltpu.VMEM((2, 8, TOK), F32),
             pltpu.VMEM((4, 2, BLOCK, SLAB), BF16),
             pltpu.VMEM((4, 2, 8, 2, CAP, SLAB), BF16),
             pltpu.VMEM((8, 8, 4, CAP, 256), BF16),
@@ -565,16 +638,16 @@
             pltpu.VMEM((8, 64, 128), F32),
             pltpu.VMEM((8, 8, 128), F32),
             pltpu.VMEM((8, 8, 128), F32),
+            pltpu.VMEM((2, 128), F32),
+            pltpu.VMEM((4, 2, 128), F32),
             pltpu.VMEM((2, 64, TOK), F32),
             pltpu.VMEM((8, 8, TOK), F32),
             pltpu.VMEM((8, 8, TOK), F32),
             pltpu.VMEM((16, TOK), F32),
-            dma((2, 7, 2)),
-            dma((2, 7, 2)),
-            dma((2, 3)),
-            dma((2, 3)),
-            dma((2, 8)),
-            dma((2, 8)),
+            dma((2, 9, 3)),
+            dma((2, 9, 3)),
+            dma((2, 9)),
+            dma((2, 9)),
             dma((4, 2)),
             dma((4, 2)),
             dma((len(ROUNDS), 8)),
@@ -585,6 +658,8 @@
             dma((8,)),
             dma((8,)),
             dma((8,)),
+            dma((8,)),
+            dma((4,)),
             dma((3,)),
         ],
         compiler_params=pltpu.CompilerParams(

time: 120 us -> 119 us (level)
  no operation moved by 1% of the time
where the time goes in v3:
time: 119 us
  Pallas kernels  118 us (99%)
  local copies, waits for them, and re-layouts  1.24 us (1%)
    pallas_call x1, Pallas kernels, per_device(): pl.pallas_call(kernel, out_shape=jax.ShapeDtypeStruct((1, TOK), F32), in_...  118 us

profile of v3, /device:TPU:1, one launch (start us, length us, event | category | flops | bytes accessed | tf_op | source)
XLA Modules:
  0.0 119.2 jit_solution(4591126360054615675)
XLA Ops:
  0.0 117.9 %shard_map.64 = f32[1,256]{1,0:T(1,128)} custom-call(bf16[256,1024]{1,0:T(8,128)(2,1)} %hid.1, f32[1,1024]{1,0:T(1,128)} %bitcast.4, bf16[1024,1024]{1,0:T(8,128)(2,1)} %head.1, s32[4,256]{1,0:T(4,128)} %allowed.1, s32[1,256]{1,0:T(1,128)} %bitcast.6, s32[1,256]{1,0:T(1,128)} %bitcast.7), custom_call_target="tpu_custom_call" | custom-call | tf_op jit(solution)/shard_map/pallas_call | solution.py:623
  117.9 1.2 %copy.8 = f32[256]{0:T(256)} copy(f32[256]{0:T(256)} %bitcast.5) | data formatting | bytes 2048

commit v4 on v3

--- a/solution.py
+++ b/solution.py
@@ -20,7 +20,7 @@
 ROUND_A = ((0, 2, 1, 4, None), (0, 2, 0, 1, 0))
 ROUND_B = ((0, 2, 4, 6, None), (2, 3, 1, 6, None), (2, 3, 0, 1, 0))
 ROUND_C = ((0, 3, 6, 7, None), (3, 4, 1, 7, None), (3, 4, 0, 1, 0))
-ROUND_D = ((0, 4, 7, 8, None),)
+ROUND_D = ((0, 2, 7, 8, None), (2, 4, 7, 8, None))
 ROUND_E = ((0, 2, 0, 1, 1), (2, 4, 0, 1, 1))
 ROUNDS = ROUND_A + ROUND_B + ROUND_C + ROUND_D + ROUND_E
 
@@ -47,6 +47,7 @@
     Rr,
     Qs,
     Qr,
+    table,
     rcode,
     Sx,
     E,
@@ -421,6 +422,15 @@
     for c in own_head:
         c.wait()
 
+    for n in range(3):
+        shift = ((lax.rem(z + (7, 9, 8)[n], NZ) - z) * 128).astype(F32)
+        for i in range(2):
+            rows = rcode[i] + shift
+            for j in range(A):
+                table[n, i, :, pl.ds(j * TOK, TOK)] = jnp.where(
+                    rows == named[j : j + 1], 1.0, 0.0
+                )
+
     for k in range(1, 6):
         for d in range(2):
             slab(k, d, 0).wait_recv()
@@ -479,49 +489,60 @@
         slab(7, d, 2).wait_recv()
     for d in range(2):
         gather(7, d)
-    products_flat(0, 4, 7)
+    products_flat(0, 2, 7)
     send((8,))
+    products_flat(2, 4, 7)
+    send((9,))
 
     for d in range(2):
         slab(8, d, 0).wait_recv()
         meta(8, d).wait_recv()
     gather_last()
     products_last(0, 2)
-    send((9,))
+    send((10,))
     products_last(2, 4)
-    send((10,))
+    send((11,))
 
     stats((5, 6, 7))
     for k in range(1, 7):
         turn(k)
         report(k).start()
-    stats((8,))
-    turn(7)
-    report(7).start()
-
-    def finish(rel):
-        return push(
-            Qs, Qr.at[2 * my_i + my_h], qs.at[rel], qr.at[2 * my_i + my_h],
-            lax.rem(seg + rel, 8), at_z(8),
-        )
 
     @pl.when(my_d == 0)
     def _():
         turn(0)
         Rr[0] = Rs[0]
 
-    stats((9, 10))
+    def finish(n, rel):
+        step = 8 if n == 2 else jnp.where(my_d == 0, -7, 7)
+        place = n if n == 2 else my_d
+        quarter = 2 * my_i + my_h
+        return push(
+            Qs.at[n // 2],
+            Qr.at[place, quarter],
+            qs.at[n // 2, rel],
+            qr.at[place, quarter],
+            lax.rem(seg + rel, 8),
+            at_z(step),
+        )
+
+    def give(n, k):
+        rows = St[k]
+        turned = jnp.concatenate([rows, rows], axis=0).T
+        lane = lax.broadcasted_iota(jnp.int32, (1, 128), 1)
+        Qs[n // 2] = jnp.concatenate(
+            [jnp.where(lane < 64, turned[0:1], turned[1:2]), turned[2:3]], axis=0
+        )
+        for rel in range(8):
+            finish(n, rel).start()
+
+    stats((8, 9))
+    give(0, 7)
+    stats((10, 11))
 
     @pl.when(my_d == 1)
     def _():
-        rows = St[0]
-        turned = jnp.concatenate([rows, rows], axis=0).T
-        lane = lax.broadcasted_iota(jnp.int32, (1, 128), 1)
-        Qs[...] = jnp.concatenate(
-            [jnp.where(lane < 64, turned[0:1], turned[1:2]), turned[2:3]], axis=0
-        )
-        for rel in range(8):
-            finish(rel).start()
+        give(2, 0)
 
     for k in range(1, 9):
         for d in range(2):
@@ -532,7 +553,7 @@
         square(rel).wait_send()
     sent(range(len(ROUNDS)))
 
-    for k in range(1, 8):
+    for k in range(1, 7):
         report(k).wait_recv()
         collect(k, jnp.where(my_d == 0, k, -k))
 
@@ -559,61 +580,61 @@
 
     for rel in range(1, 8):
         share(rel).start()
-    for k in range(1, 8):
+    for k in range(1, 7):
         report(k).wait_send()
 
     for rel in range(1, 8):
         share(rel).wait_recv()
-    for n in range(4):
-        push(Qs, Qr.at[n], qs.at[n], qr.at[n], seg, at_z(8)).wait_recv()
-
-    stacked = jnp.concatenate([Qr[n] for n in range(4)], axis=0)
-    columns = jnp.concatenate([stacked] * 16, axis=0).T
-    last = []
-    plane = ((lax.rem(z + 8, NZ) - z) * 128).astype(F32)
-    for i in range(2):
-        first, second = 4 * i, 4 * i + 2
-        peaks = [columns[0:64, n : n + 1] for n in (first, second)]
-        peak = jnp.maximum(peaks[0], peaks[1])
-        mass = columns[64:128, first : first + 1] * jnp.exp(peaks[0] - peak)
-        mass = mass + columns[64:128, second : second + 1] * jnp.exp(peaks[1] - peak)
-        goal = columns[0:64, first + 1 : first + 2] + columns[0:64, second + 1 : second + 2]
-        last.append((rcode[i] + plane, peak, mass, goal))
-    found = []
-    for j in range(A):
-        rows = M[0, 0, j : j + 1, :]
-        sums = [jnp.zeros((1, TOK), F32)] * 3
-        for codes_of, *values in last:
-            match = codes_of == rows
-            sums = [
-                s + jnp.sum(jnp.where(match, value, 0.0), axis=0, keepdims=True)
-                for s, value in zip(sums, values)
-            ]
-        found.append(sums)
-
+    mine = []
+    for n in range(3):
+        for quarter in range(4):
+            push(
+                Qs.at[0], Qr.at[n, quarter], qs.at[0, 0], qr.at[n, quarter], seg, at_z(8)
+            ).wait_recv()
+        got = jnp.concatenate([Qr[n, quarter] for quarter in range(4)], axis=0)
+        got = jnp.concatenate([got[:, 0:64], got[:, 64:128]], axis=0)
+        for i in range(2):
+            found = jnp.dot(
+                got,
+                table[n, i],
+                precision=lax.Precision.HIGHEST,
+                preferred_element_type=F32,
+            )
+            for h in range(2):
+                row = 4 * i + 2 * h
+                mine.append(
+                    (found[row : row + 1], found[row + 8 : row + 9], found[row + 1 : row + 2])
+                )
+    peak, mass, goal = (jnp.concatenate(rows, axis=0) for rows in zip(*mine))
+    here = mass > 0.5
+    marked_peak = jnp.where(here, peak, -1e30)
+    best = jnp.max(marked_peak, axis=0, keepdims=True)
+    top_here = functools.reduce(
+        jnp.maximum, [best[:, j * TOK : (j + 1) * TOK] for j in range(A)]
+    )
     top = E[0, 0:1]
     for rel in range(1, 8):
         top = jnp.maximum(top, E[rel, 0:1])
-    for peak, mass, _ in found:
-        top = jnp.maximum(top, jnp.where(mass > 0.5, peak, -1e30))
-    mass = jnp.zeros((1, TOK), F32)
-    goal = jnp.zeros((1, TOK), F32)
+    top = jnp.maximum(top, top_here)
+    weight = jnp.exp(marked_peak - jnp.concatenate([top] * A, axis=1))
+    mass_here = jnp.sum(jnp.where(here, mass * weight, 0.0), axis=0, keepdims=True)
+    goal_here = jnp.sum(goal, axis=0, keepdims=True)
+    mass = sum(mass_here[:, j * TOK : (j + 1) * TOK] for j in range(A))
+    goal = sum(goal_here[:, j * TOK : (j + 1) * TOK] for j in range(A))
     for rel in range(8):
         mass = mass + E[rel, 1:2] * jnp.exp(E[rel, 0:1] - top)
         goal = goal + E[rel, 2:3]
-    for a_peak, a_mass, a_goal in found:
-        here = a_mass > 0.5
-        weight = jnp.exp(jnp.where(here, a_peak - top, 0.0))
-        mass = mass + jnp.where(here, a_mass * weight, 0.0)
-        goal = goal + a_goal
     out[...] = goal - (top + jnp.log(mass))
     for rel in range(1, 8):
         share(rel).wait_send()
 
+    for rel in range(8):
+        finish(0, rel).wait_send()
+
     @pl.when(my_d == 1)
     def _():
         for rel in range(8):
-            finish(rel).wait_send()
+            finish(2, rel).wait_send()
 
 
 def per_device(hidden, norm_gain, head, allowed, target_slot, target_offset):
@@ -638,8 +659,9 @@
             pltpu.VMEM((8, 64, 128), F32),
             pltpu.VMEM((8, 8, 128), F32),
             pltpu.VMEM((8, 8, 128), F32),
-            pltpu.VMEM((2, 128), F32),
-            pltpu.VMEM((4, 2, 128), F32),
+            pltpu.VMEM((2, 2, 128), F32),
+            pltpu.VMEM((3, 4, 2, 128), F32),
+            pltpu.VMEM((3, 2, 64, A * TOK), F32),
             pltpu.VMEM((2, 64, TOK), F32),
             pltpu.VMEM((8, 8, TOK), F32),
             pltpu.VMEM((8, 8, TOK), F32),
@@ -658,8 +680,8 @@
             dma((8,)),
             dma((8,)),
             dma((8,)),
-            dma((8,)),
-            dma((4,)),
+            dma((2, 8)),
+            dma((3, 4)),
             dma((3,)),
         ],
         compiler_params=pltpu.CompilerParams(

time: 119 us -> 118 us (level)
    pallas_call x1, Pallas kernels: 118 us -> 117 us  [per_device(): pl.pallas_call(kernel, out_shape=jax.ShapeDtypeStruct((1, TOK), F32), in_...]
where the time goes in v4:
time: 118 us
  Pallas kernels  117 us (99%)
  local copies, waits for them, and re-layouts  1.24 us (1%)
    pallas_call x1, Pallas kernels, per_device(): pl.pallas_call(kernel, out_shape=jax.ShapeDtypeStruct((1, TOK), F32), in_...  117 us

profile of v4, /device:TPU:1, one launch (start us, length us, event | category | flops | bytes accessed | tf_op | source)
XLA Modules:
  0.0 117.9 jit_solution(16207102221792685761)
XLA Ops:
  0.0 116.6 %shard_map.64 = f32[1,256]{1,0:T(1,128)} custom-call(bf16[256,1024]{1,0:T(8,128)(2,1)} %hid.1, f32[1,1024]{1,0:T(1,128)} %bitcast.4, bf16[1024,1024]{1,0:T(8,128)(2,1)} %head.1, s32[4,256]{1,0:T(4,128)} %allowed.1, s32[1,256]{1,0:T(1,128)} %bitcast.6, s32[1,256]{1,0:T(1,128)} %bitcast.7), custom_call_target="tpu_custom_call" | custom-call | tf_op jit(solution)/shard_map/pallas_call | solution.py:644
  116.6 1.2 %copy.8 = f32[256]{0:T(256)} copy(f32[256]{0:T(256)} %bitcast.5) | data formatting | bytes 2048

commit v5 on v4

--- a/solution.py
+++ b/solution.py
@@ -23,6 +23,7 @@
 ROUND_D = ((0, 2, 7, 8, None), (2, 4, 7, 8, None))
 ROUND_E = ((0, 2, 0, 1, 1), (2, 4, 0, 1, 1))
 ROUNDS = ROUND_A + ROUND_B + ROUND_C + ROUND_D + ROUND_E
+PAIRED = 6
 
 
 def kernel(
@@ -48,6 +49,9 @@
     Qs,
     Qr,
     table,
+    Lm,
+    Ls,
+    Lr,
     rcode,
     Sx,
     E,
@@ -306,6 +310,25 @@
                 for h in range(2):
                     Pp[4 * i + 2 * h + 1, 0, w] = logits[:, 256 * h : 256 * (h + 1)]
 
+    def products_pair():
+        for i in range(2):
+            rows = G[3, i, pl.ds(0, 7)].reshape(7 * 2 * CAP, SLAB)
+            logits = multiply(rows, 3, i).reshape(7, 2, CAP, BLOCK)
+            mine = jnp.where(my_d == 0, logits[1:7, 0], logits[1:7, 1])
+            others = jnp.where(my_d == 0, logits[1:7, 1], logits[1:7, 0])
+            for h in range(2):
+                span = slice(256 * h, 256 * (h + 1))
+                Lm[2 * i + h] = mine[:, :, span]
+                Ls[2 * i + h] = others[:, :, span]
+                Pp[4 * i + 2 * h, 0, 3] = logits[0, 0, :, span].astype(BF16)
+
+    def pair():
+        return push(Ls, Lr, own.at[3], own.at[4], seg + 1 - 2 * my_d, v)
+
+    def add_pair():
+        for n in range(4):
+            Pp[2 * n + my_d, 1:7, 3] = (Lm[n] + Lr[n]).astype(BF16)
+
     def partial(r, rel):
         w0, w1, k0, k1, _ = ROUNDS[r]
         dest = lax.rem(seg + rel, 8)
@@ -322,6 +345,11 @@
     def each_peer(r, act):
         side = ROUNDS[r][4]
 
+        if r == PAIRED:
+            for rel in (2, 4, 6):
+                act(partial(r, rel))
+            return
+
         def one(rel, carry):
             if side is None:
                 act(partial(r, rel))
@@ -359,14 +387,18 @@
             partial(r, rel).wait_recv()
             return carry
 
-        lax.fori_loop(1, 8, arrive, 0)
+        if r == PAIRED:
+            for rel in (2, 4, 6):
+                partial(r, rel).wait_recv()
+        else:
+            lax.fori_loop(1, 8, arrive, 0)
 
         last = r >= len(ROUNDS) - len(ROUND_E)
 
         def one(k, carry):
             span = pl.ds(w0, w1 - w0)
             logits = Pp[seg, k, span].reshape(n, 256).astype(F32)
-            for rel in range(1, 8):
+            for rel in (2, 4, 6) if r == PAIRED else range(1, 8):
                 logits = logits + Pr[rel, k, span].reshape(n, 256).astype(F32)
             info = M[my_i if last else my_d, 8 if last else k]
             rows = rcode[my_i, pl.ds(w0 * CAP, n), :]
@@ -442,20 +474,20 @@
             slab(k + 1, d, 1).start()
         for d in range(2):
             gather(k, d)
-        if k == 2:
+        if k == 1:
+            for i in range(2):
+                block(2, i).start()
+        if k == 3:
             for i in range(2):
                 block(1, i).wait()
-                block(2, i).start()
-        if k == 3:
+                block(3, i).start()
             products(0, 2, 0, 4)
             send((0, 1))
-        if k == 4:
-            for i in range(2):
-                block(2, i).wait()
-                block(3, i).start()
         if k == 5:
             products(0, 2, 4, 6)
             send((2,))
+            for i in range(2):
+                block(2, i).wait()
             products(2, 3, 0, 6)
             send((3, 4))
             stats((0, 1))
@@ -480,9 +512,13 @@
         slab(8, d, 0).start()
     for i in range(2):
         block(3, i).wait()
-    products(3, 4, 0, 7)
-    send((6, 7))
+    products_pair()
+    pair().start()
+    send((7,))
     stats((2, 3, 4))
+    pair().wait()
+    add_pair()
+    send((PAIRED,))
 
     for d in range(2):
         slab(7, d, 1).wait_recv()
@@ -662,6 +698,9 @@
             pltpu.VMEM((2, 2, 128), F32),
             pltpu.VMEM((3, 4, 2, 128), F32),
             pltpu.VMEM((3, 2, 64, A * TOK), F32),
+            pltpu.VMEM((4, 6, CAP, 256), F32),
+            pltpu.VMEM((4, 6, CAP, 256), F32),
+            pltpu.VMEM((4, 6, CAP, 256), F32),
             pltpu.VMEM((2, 64, TOK), F32),
             pltpu.VMEM((8, 8, TOK), F32),
             pltpu.VMEM((8, 8, TOK), F32),
@@ -682,7 +721,7 @@
             dma((8,)),
             dma((2, 8)),
             dma((3, 4)),
-            dma((3,)),
+            dma((5,)),
         ],
         compiler_params=pltpu.CompilerParams(
             collective_id=0, has_side_effects=True, vmem_limit_bytes=56 * 2**20

time: 118 us -> 118 us (level)
  no operation moved by 1% of the time
where the time goes in v5:
time: 118 us
  Pallas kernels  117 us (99%)
  local copies, waits for them, and re-layouts  1.24 us (1%)
    pallas_call x1, Pallas kernels, per_device(): pl.pallas_call(kernel, out_shape=jax.ShapeDtypeStruct((1, TOK), F32), in_...  117 us

profile of v5, /device:TPU:1, one launch (start us, length us, event | category | flops | bytes accessed | tf_op | source)
XLA Modules:
  0.0 117.8 jit_solution(1839383332109463533)
XLA Ops:
  0.0 116.6 %shard_map.64 = f32[1,256]{1,0:T(1,128)} custom-call(bf16[256,1024]{1,0:T(8,128)(2,1)} %hid.1, f32[1,1024]{1,0:T(1,128)} %bitcast.4, bf16[1024,1024]{1,0:T(8,128)(2,1)} %head.1, s32[4,256]{1,0:T(4,128)} %allowed.1, s32[1,256]{1,0:T(1,128)} %bitcast.6, s32[1,256]{1,0:T(1,128)} %bitcast.7), custom_call_target="tpu_custom_call" | custom-call | tf_op jit(solution)/shard_map/pallas_call | solution.py:680
  116.6 1.2 %copy.8 = f32[256]{0:T(256)} copy(f32[256]{0:T(256)} %bitcast.5) | data formatting | bytes 2048

commit v6 on v5

--- a/solution.py
+++ b/solution.py
@@ -530,6 +530,11 @@
     products_flat(2, 4, 7)
     send((9,))
 
+    stats((5, 6, 7))
+    for k in range(1, 7):
+        turn(k)
+        report(k).start()
+
     for d in range(2):
         slab(8, d, 0).wait_recv()
         meta(8, d).wait_recv()
@@ -539,10 +544,6 @@
     products_last(2, 4)
     send((11,))
 
-    stats((5, 6, 7))
-    for k in range(1, 7):
-        turn(k)
-        report(k).start()
 
     @pl.when(my_d == 0)
     def _():

time: 118 us -> 122 us (1.034)
  Pallas kernels: 117 us -> 120 us
    pallas_call x1, Pallas kernels: 117 us -> 120 us  [per_device(): pl.pallas_call(kernel, out_shape=jax.ShapeDtypeStruct((1, TOK), F32), in_...]
where the time goes in v6:
time: 122 us; the launch traced here: 121 us
  Pallas kernels  120 us (98%)
  local copies, waits for them, and re-layouts  1.24 us (1%)
    pallas_call x1, Pallas kernels, per_device(): pl.pallas_call(kernel, out_shape=jax.ShapeDtypeStruct((1, TOK), F32), in_...  120 us

profile of v6, /device:TPU:1, one launch (start us, length us, event | category | flops | bytes accessed | tf_op | source)
XLA Modules:
  0.0 121.4 jit_solution(11313696584596195531)
XLA Ops:
  0.0 120.2 %shard_map.64 = f32[1,256]{1,0:T(1,128)} custom-call(bf16[256,1024]{1,0:T(8,128)(2,1)} %hid.1, f32[1,1024]{1,0:T(1,128)} %bitcast.4, bf16[1024,1024]{1,0:T(8,128)(2,1)} %head.1, s32[4,256]{1,0:T(4,128)} %allowed.1, s32[1,256]{1,0:T(1,128)} %bitcast.6, s32[1,256]{1,0:T(1,128)} %bitcast.7), custom_call_target="tpu_custom_call" | custom-call | tf_op jit(solution)/shard_map/pallas_call | solution.py:681
  120.2 1.2 %copy.8 = f32[256]{0:T(256)} copy(f32[256]{0:T(256)} %bitcast.5) | data formatting | bytes 2048
